TPU v7x, 32 devices: a whole 2x2x4 slice. The times are simulated.
32 devices in a mesh: groups: 2 (over y), expert: 4 (over x, core), fsdp: 4 (over z).
Axes of the slice: x: 2, y: 2, z: 4, core: 2. Of those that a mesh axis runs over, the one named last changes fastest.
Arguments:
- tokens: bfloat16 [32768, 512], P(('groups', 'expert', 'fsdp')), parts along dimension 0, may hold values from -6 to 6
- routes: int32 [32768], P(('groups', 'expert', 'fsdp')), parts along dimension 0, may hold values from 0 to 7, as said below
- slot_ids: int32 [32768], P(('groups', 'expert', 'fsdp')), parts along dimension 0, may hold values from 0 to 159, as said below
- qkv_weight: bfloat16 [512, 1536], P('fsdp'), may hold values from -0.25 to 0.25
- proj_weight: bfloat16 [512, 512], P('fsdp'), may hold values from -0.25 to 0.25
- logit_scale: float32 [16], replicated, may hold values from 1.5 to 5.5
- bias_network_first_weight: float32 [2, 512], P(None, 'fsdp'), may hold values from -4 to 4
- bias_network_first_offset: float32 [512], P('fsdp'), may hold values from -3 to 3
- bias_network_second_weight: float32 [512, 16], P('fsdp'), may hold values from -0.25 to 0.25
- attn_gain: float32 [512], replicated, may hold values from 0.1 to 1.9
- router: bfloat16 [512, 8], replicated, may hold values from -0.25 to 0.25
- moe_gain: float32 [512], replicated, may hold values from 0.1 to 1.9
- expert_in: bfloat16 [8, 512, 2048], P('expert'), may hold values from -0.25 to 0.25
- expert_out: bfloat16 [8, 2048, 512], P('expert'), may hold values from -0.125 to 0.125
Outputs:
- block_out: bfloat16 [32768, 512], P(('groups', 'expert', 'fsdp')), parts along dimension 0
There are 2 independent parts, one for each index of `groups`. A program takes and returns all parts, laid end to end along the dimension named above; an argument that names none is the same for every part. Nothing has to cross between parts.
Inputs may be any that keep to these rules, and one draw needn't show every extreme that they name: `routes`: each device's 1024 tokens name every expert at most 160 times; one expert, the same on every device, is named exactly 160 times by each device's tokens. `slot_ids`: among one device's tokens with the same route, the slots are distinct.
All inputs are finite; a program needn't handle non-finite values.
Results may differ from a plain program's by a relative error of at most 0.012.
The roundings to bfloat16 on the way count: a program that leaves them out, or rounds other values in their place, can miss the bound.
Values may be sent and summed in bfloat16 or wider, within the bound.
A program may use at most 192 MiB of HBM per device.

v0:
```python
import functools
import math

import jax
import jax.numpy as jnp
import numpy as np
from jax import lax
from jax.experimental import pallas as pl
from jax.experimental.pallas import tpu as pltpu
from jax.sharding import PartitionSpec as P

HEADS = 16
WIN = 16
WTOK = WIN * WIN
LOG2E = math.log2(math.e)
NORM_EPS = 1e-05
UNIT_EPS = 1e-06
HIGHEST = lax.Precision.HIGHEST
MIB = 1024 * 1024
F32 = jnp.float32
BF16 = jnp.bfloat16


def table_coords():
    offsets = (WIN - 1 - np.arange(32)).astype(np.float32)
    stretched = offsets / np.float32(WIN - 1) * np.float32(8.0)
    logged = np.sign(stretched) * np.log2(np.abs(stretched) + np.float32(1.0)) / np.float32(3.0)
    logged = logged.astype(np.float32)
    out = np.zeros((1024, 8), np.float32)
    out[:, 0] = np.repeat(logged, 32)
    out[:, 1] = np.tile(logged, 32)
    return out


def layer_norm(values, gain):
    centre = values - jnp.mean(values, axis=-1, keepdims=True)
    spread = jnp.mean(centre * centre, axis=-1, keepdims=True)
    return centre * lax.rsqrt(spread + NORM_EPS) * gain


def dot(a, b):
    return jnp.dot(a, b, preferred_element_type=F32)


def dot_nt(a, b, precision=None):
    return lax.dot_general(
        a, b, (((1,), (1,)), ((), ())), precision=precision, preferred_element_type=F32
    )


def build_bias(net_ref, coords_ref, strips, bias):
    shard_count = net_ref.shape[0]
    c0 = coords_ref[:, 0:1]
    c1 = coords_ref[:, 1:2]
    table = None
    for z in range(shard_count):
        hidden = c0 * net_ref[z, 16:17, :] + c1 * net_ref[z, 17:18, :] + net_ref[z, 18:19, :]
        hidden = jnp.maximum(hidden, 0.0)
        part = dot_nt(net_ref[z, 0:16, :], hidden, HIGHEST)
        table = part if table is None else table + part
    table = (16.0 * LOG2E) * jax.nn.sigmoid(table)
    stacked = jnp.concatenate([table[:, g * 256 : (g + 1) * 256] for g in range(4)], axis=0)
    high = stacked.astype(BF16)
    rest = stacked - high.astype(F32)
    mid = rest.astype(BF16)
    low = (rest - mid.astype(F32)).astype(BF16)
    pieces = jnp.concatenate([high, mid, low], axis=0)
    k = lax.broadcasted_iota(jnp.int32, (256, 128), 0)
    c = lax.broadcasted_iota(jnp.int32, (256, 128), 1)
    same_row = (k // 32) == (c // 16)
    shift = (k % 32) - (c % 16)
    for xi in range(16):
        sel = jnp.where(same_row & (shift == 15 - xi), 1.0, 0.0).astype(BF16)
        picked = dot(pieces, sel)
        strips[xi] = picked[0:64] + picked[64:128] + picked[128:192]
    for h in range(HEADS):
        strip = jnp.concatenate([strips[:, g * 16 + h, :] for g in range(4)], axis=1)
        for yi in range(16):
            start = (15 - yi) * 16
            bias[h, yi * 16 : (yi + 1) * 16, :] = strip[:, start : start + 256]


def attention_kernel(
    tok_ref, wqkv_ref, wproj_ref, net_ref, coords_ref, ls_ref, ag_ref, mg_ref,
    res_ref, normed_ref, strips, bias, ones_ref, ctx_ref,
):
    @pl.when(pl.program_id(0) == 0)
    def _():
        build_bias(net_ref, coords_ref, strips, bias)
        r = lax.broadcasted_iota(jnp.int32, ones_ref.shape, 0)
        c = lax.broadcasted_iota(jnp.int32, ones_ref.shape, 1)
        ones_ref[...] = jnp.where((r // 32) == (c // 32), 1.0, 0.0).astype(BF16)

    width = tok_ref.shape[1]
    tok = tok_ref[...]
    scales = jnp.exp(jnp.minimum(ls_ref[...], math.log(100.0))) * LOG2E
    lane = lax.broadcasted_iota(jnp.int32, (WTOK, 128), 1) // 32

    def unit(col):
        x = dot(tok, wqkv_ref[:, col : col + 256])
        sq = x * x
        high = sq.astype(BF16)
        low = (sq - high.astype(F32)).astype(BF16)
        ones = ones_ref[...]
        total = dot(high, ones) + dot(low, ones)
        return (x * lax.rsqrt(total + UNIT_EPS)).astype(BF16)

    for pair in range(width // 256):
        base = pair * 256
        uq2 = unit(base)
        uk2 = unit(width + base)
        v2 = dot(tok, wqkv_ref[:, 2 * width + base : 2 * width + base + 256]).astype(BF16)
        for half in range(2):
            uq = uq2[:, half * 128 : (half + 1) * 128]
            uk = uk2[:, half * 128 : (half + 1) * 128]
            v = v2[:, half * 128 : (half + 1) * 128]
            ctx = None
            for j in range(4):
                h = pair * 8 + half * 4 + j
                q = jnp.where(lane == j, uq, jnp.zeros_like(uq))
                s = dot_nt(q, uk) * scales[:, h : h + 1] + bias[h]
                e = jnp.exp2(s - jnp.max(s, axis=-1, keepdims=True))
                w = (e * (1.0 / jnp.sum(e, axis=-1, keepdims=True))).astype(BF16)
                o = dot(w, v)
                ctx = o if ctx is None else jnp.where(lane == j, o, ctx)
            ctx_ref[:, base + half * 128 : base + (half + 1) * 128] = ctx.astype(BF16)

    attended = dot(ctx_ref[...], wproj_ref[...])
    residual = tok.astype(F32) + layer_norm(attended, ag_ref[...])
    res_ref[...] = residual
    normed_ref[...] = layer_norm(residual, mg_ref[...]).astype(BF16)


def whole_block(shape):
    return pl.BlockSpec(shape, lambda i: (0,) * len(shape))


def attention(tokens, wqkv, wproj, net, logit_scale, attn_gain, moe_gain):
    rows, width = tokens.shape
    coords = jnp.asarray(table_coords())
    rows_block = pl.BlockSpec((WTOK, width), lambda i: (i, 0))
    return pl.pallas_call(
        attention_kernel,
        grid=(rows // WTOK,),
        out_shape=(
            jax.ShapeDtypeStruct((rows, width), F32),
            jax.ShapeDtypeStruct((rows, width), BF16),
        ),
        in_specs=[
            rows_block,
            whole_block(wqkv.shape),
            whole_block(wproj.shape),
            whole_block(net.shape),
            whole_block(coords.shape),
            whole_block((1, HEADS)),
            whole_block((1, width)),
            whole_block((1, width)),
        ],
        out_specs=(rows_block, rows_block),
        scratch_shapes=[
            pltpu.VMEM((16, 64, 128), F32),
            pltpu.VMEM((HEADS, WTOK, WTOK), F32),
            pltpu.VMEM((256, 256), BF16),
            pltpu.VMEM((WTOK, width), BF16),
        ],
        compiler_params=pltpu.CompilerParams(vmem_limit_bytes=48 * MIB),
        name="attention",
    )(
        tokens, wqkv, wproj, net, coords, logit_scale.reshape(1, HEADS),
        attn_gain.reshape(1, width), moe_gain.reshape(1, width),
    )


def combine_kernel(cap, res_ref, normed_ref, router_ref, routes_ref, slots_ref, ret_ref, out_ref):
    rows = res_ref.shape[0]
    slots = ret_ref.shape[0]
    eye = lax.broadcasted_iota(jnp.int32, (rows, rows), 0) == lax.broadcasted_iota(
        jnp.int32, (rows, rows), 1
    )

    def column(row):
        wide = jnp.where(eye, row.astype(F32), 0.0)
        return jnp.sum(wide, axis=1, keepdims=True).astype(jnp.int32)

    routes = column(routes_ref[...])
    place = column(routes_ref[...] * cap + slots_ref[...])
    logits = dot(normed_ref[...], router_ref[...])
    expert = lax.broadcasted_iota(jnp.int32, logits.shape, 1)
    picked = jnp.sum(jnp.where(expert == routes, logits, 0.0), axis=1, keepdims=True)
    gate = jax.nn.sigmoid(picked)
    spot = lax.broadcasted_iota(jnp.int32, (rows, slots), 1)
    one_hot = jnp.where(spot == place, 1.0, 0.0).astype(BF16)
    out_ref[...] = (res_ref[...] + gate * dot(one_hot, ret_ref[...])).astype(BF16)


def combine(residual, normed, router, routes, slot_ids, returned, cap):
    rows, width = residual.shape
    step = WTOK
    rows_block = pl.BlockSpec((step, width), lambda i: (i, 0))
    ids_block = pl.BlockSpec((1, step), lambda i: (0, i))
    return pl.pallas_call(
        functools.partial(combine_kernel, cap),
        grid=(rows // step,),
        out_shape=jax.ShapeDtypeStruct((rows, width), BF16),
        in_specs=[
            rows_block, rows_block, whole_block(router.shape), ids_block, ids_block,
            whole_block(returned.shape),
        ],
        out_specs=rows_block,
        compiler_params=pltpu.CompilerParams(vmem_limit_bytes=48 * MIB),
        name="combine",
    )(residual, normed, router, routes.reshape(1, rows), slot_ids.reshape(1, rows), returned)


def run_experts(arrived, first_weight, second_weight):
    inner = jnp.einsum("secd,edf->secf", arrived, first_weight, preferred_element_type=F32)
    inner = jax.nn.gelu(inner, approximate=False).astype(BF16)
    return jnp.einsum("secf,efd->secd", inner, second_weight, preferred_element_type=F32).astype(BF16)


def shards(
    tokens, routes, slot_ids, qkv_weight, proj_weight, logit_scale, first_weight, first_offset,
    second_weight, attn_gain, router, moe_gain, expert_in, expert_out,
):
    rows, width = tokens.shape
    units = first_weight.shape[1]
    net = jnp.concatenate(
        [second_weight.T, first_weight, first_offset[None], jnp.zeros((5, units), F32)], axis=0
    )
    net = lax.all_gather(net, "fsdp", axis=0)
    wqkv = lax.all_gather(qkv_weight, "fsdp", axis=0, tiled=True)
    wproj = lax.all_gather(proj_weight, "fsdp", axis=0, tiled=True)
    residual, normed = attention(tokens, wqkv, wproj, net, logit_scale, attn_gain, moe_gain)
    experts = router.shape[1]
    held = expert_in.shape[0]
    ranks = lax.axis_size("expert")
    cap = rows * 5 // (4 * experts)
    column = routes * cap + slot_ids
    one_hot = (column[:, None] == jnp.arange(experts * cap, dtype=jnp.int32)[None, :]).astype(BF16)
    packed = lax.dot_general(
        one_hot, normed, (((0,), (0,)), ((), ())), preferred_element_type=F32
    ).astype(BF16)
    arrived = lax.all_to_all(
        packed.reshape(ranks, held, cap, width), "expert", split_axis=0, concat_axis=0, tiled=True
    )
    answers = run_experts(arrived, expert_in, expert_out)
    returned = lax.all_to_all(answers, "expert", split_axis=0, concat_axis=0, tiled=True)
    returned = returned.reshape(experts * cap, width)
    return combine(residual, normed, router, routes, slot_ids, returned, cap)


def solution(mesh):
    rows = P(("groups", "expert", "fsdp"))
    return jax.shard_map(
        shards,
        mesh=mesh,
        in_specs=(
            P(("groups", "expert", "fsdp"), None), rows, rows, P("fsdp", None), P("fsdp", None),
            P(), P(None, "fsdp"), P("fsdp"), P("fsdp", None), P(), P(), P(),
            P("expert", None, None), P("expert", None, None),
        ),
        out_specs=P(("groups", "expert", "fsdp"), None),
        check_vma=False,
    )
```

profile of v0, /device:TPU:1, one launch (start us, length us, event | category | flops | bytes accessed | tf_op | source)
XLA Modules:
  0.0 165.4 jit_solution(2614165911617766944)
XLA Ops:
  6.5 0.7 all-gather.3.cloned.1.call-update
  7.3 0.1 pad.3.clone
  7.3 0.8 maximum_maximum_fusion
  8.1 11.6 %all-gather = f32[96,128]{1,0:T(8,128)S(1)} all-gather(f32[24,128]{1,0:T(8,128)S(1)} %maximum_maximum_fusion), channel_id=2, replica_groups=mesh['groups'=2,'expert'=4,'fsdp'=4] {'fsdp'}, dimensions={0}, use_global_device_ids=true | all-gather | bytes 61440 | tf_op jit(solution)/shard_map/all_gather | solution.py:230
  19.8 20.3 %all_gather.13.wproj_ref = bf16[512,512]{1,0:T(8,128)(2,1)S(1)} all-gather(bf16[128,512]{1,0:T(8,128)(2,1)} %param.19), channel_id=1, replica_groups=mesh['groups'=2,'expert'=4,'fsdp'=4] {'fsdp'}, dimensions={0}, use_global_device_ids=true | all-gather | bytes 655360 | tf_op jit(solution)/shard_map/all_gather | solution.py:232
  40.1 0.7 multiply_add_fusion
  40.8 15.7 %all-gather.3.cloned.1.call-done.wqkv_ref = bf16[512,1536]{1,0:T(8,128)(2,1)} async-done(((bf16[128,1536]{1,0:T(8,128)(2,1)}), bf16[512,1536]{1,0:T(8,128)(2,1)}) %all-gather.3.cloned.1.call-update) | async-done | bytes 1572880 | tf_op jit(solution)/shard_map/all_gather | solution.py:231
  56.5 1.4 copy-done.1
  57.9 1.2 copy-done.2
  59.1 1.0 copy-done.5
  60.2 0.7 copy-done.8
  60.9 0.7 copy-done.9
  61.6 0.7 copy-done.10
  62.2 20.9 %attention.1 = (f32[1024,512]{1,0:T(8,128)}, bf16[1024,512]{1,0:T(8,128)(2,1)S(1)}) custom-call(bf16[1024,512]{1,0:T(8,128)(2,1)S(1)} %copy-done.2, bf16[512,1536]{1,0:T(8,128)(2,1)S(1)} %copy-done.1, bf16[512,512]{1,0:T(8,128)(2,1)S(1)} %all_gather.13.wproj_ref, f32[4,24,128]{2,1,0:T(8,128)S(1)} %bitcast.109, f32[1024,8]{1,0:T(8,128)S(1)} %copy-done.5, ...), custom_call_target="tpu_custom_call" | custom-call | tf_op jit(solution)/shard_map/attention/pallas_call | solution.py:142
  83.1 1.9 %fusion.28 = bf16[1280,512]{1,0:T(8,128)(2,1)S(1)} fusion(bf16[1024,512]{1,0:T(8,128)(2,1)S(1)} %get-tuple-element.8.normed_ref, s32[1024]{0:T(1024)S(1)} %multiply_add_fusion), kind=kOutput, calls=%fused_computation.30 | convolution fusion | flops 1344143360 | bytes 2363392 | tf_op jit(solution)/shard_map/dot_general | solution.py:240
  84.9 19.5 %all_to_all.10 = bf16[4,2,160,512]{3,2,1,0:T(8,128)(2,1)S(1)} all-to-all(bf16[4,2,160,512]{3,2,1,0:T(8,128)(2,1)S(1)} %bitcast.115), channel_id=1, replica_groups=mesh['groups'=2,'expert'=4,'fsdp'=4] {'expert'}, dimensions={0} | all-to-all | bytes 2621440 | tf_op jit(solution)/shard_map/all_to_all | solution.py:243
  104.4 27.6 %fusion.37 = bf16[4,2,160,512]{3,2,0,1:T(8,128)(2,1)S(1)} fusion(bf16[2,2048,512]{2,1,0:T(8,128)(2,1)} %param.28, bf16[2,512,2048]{2,1,0:T(8,128)(2,1)} %param.27, bf16[4,2,160,512]{3,2,1,0:T(8,128)(2,1)S(1)} %all_to_all.10), kind=kOutput, calls=%fused_computation.33 | convolution fusion | flops 5539758080 | bytes 11010048 | tf_op jit(solution)/shard_map/secf,efd->secd/dot_general | solution.py:218
  132.0 0.0 copy-start.6
  132.0 1.2 copy.20
  133.2 4.5 %all-to-all-start.1 = ((bf16[4,2,160,512]{3,2,1,0:T(8,128)(2,1)}), bf16[4,2,160,512]{3,2,1,0:T(8,128)(2,1)S(1)}, u32[]{:S(2)}, u32[]{:S(2)}) async-start(bf16[4,2,160,512]{3,2,1,0:T(8,128)(2,1)} %copy.20), calls=%async_computation.1 | async-start | bytes 2621440 | tf_op jit(solution)/shard_map/all_to_all | solution.py:247
  137.8 0.2 copy.21.router_ref
  138.0 16.2 %all-to-all-done.1 = bf16[4,2,160,512]{3,2,1,0:T(8,128)(2,1)S(1)} async-done(((bf16[4,2,160,512]{3,2,1,0:T(8,128)(2,1)}), bf16[4,2,160,512]{3,2,1,0:T(8,128)(2,1)S(1)}, u32[]{:S(2)}, u32[]{:S(2)}) %all-to-all-start.1) | async-done | bytes 1310752 | tf_op jit(solution)/shard_map/all_to_all | solution.py:247
  154.2 1.2 copy-done.4
  155.4 3.1 %combine.1 = bf16[1024,512]{1,0:T(8,128)(2,1)} custom-call(f32[1024,512]{1,0:T(8,128)S(1)} %copy-done, bf16[1024,512]{1,0:T(8,128)(2,1)S(1)} %copy-done.4, bf16[512,8]{1,0:T(8,128)(2,1)S(1)} %copy.21.router_ref, s32[1,1024]{1,0:T(1,128)S(1)} %bitcast.110, s32[1,1024]{1,0:T(1,128)S(1)} %bitcast.111, bf16[1280,512]{1,0:T(8,128)(2,1)S(1)} %bitcast.108), custom_call_target="tpu_custom_call" | custom-call | tf_op jit(solution)/shard_map/combine/pallas_call | solution.py:201
  (18 shorter events, 0.0 us)
Async XLA Ops:
  6.5 50.0 %all-gather.3.cloned.1.call-start = ((), (), s32[]{:S(2)}) async-start(), calls=%async_computation.2 | async-start | bytes 1966080 | tf_op jit(solution)/shard_map/all_gather | solution.py:231
  56.5 1.4 copy-start.1
  57.9 1.2 copy-start.2
  59.1 1.0 copy-start.5
  60.2 0.7 copy-start.8
  60.9 0.7 copy-start.9
  61.6 0.7 copy-start.10
  83.1 1.9 %copy-start.3 = (bf16[1024,512]{1,0:T(8,128)(2,1)}, bf16[1024,512]{1,0:T(8,128)(2,1)S(1)}, u32[]{:S(2)}) copy-start(bf16[1024,512]{1,0:T(8,128)(2,1)S(1)} %get-tuple-element.8.normed_ref) | copy-start | bytes 3145732
  132.0 5.8 %copy-start.11 = (bf16[512,8]{0,1:T(8,128)(2,1)S(1)}, bf16[512,8]{0,1:T(8,128)(2,1)}, u32[]{:S(2)}) copy-start(bf16[512,8]{0,1:T(8,128)(2,1)} %param.25) | copy-start | bytes 24580
  132.0 22.2 %copy-start = (f32[1024,512]{1,0:T(8,128)S(1)}, f32[1024,512]{1,0:T(8,128)}, u32[]{:S(2)}) copy-start(f32[1024,512]{1,0:T(8,128)} %get-tuple-element.7.res_ref) | copy-start | bytes 6291460
  132.0 22.2 %copy-start.6 = (s32[1024]{0:T(1024)S(1)}, s32[1024]{0:T(1024)}, u32[]{:S(2)}) copy-start(s32[1024]{0:T(1024)} %param.16) | copy-start | bytes 12292
  132.0 22.2 %copy-start.7 = (s32[1024]{0:T(1024)S(1)}, s32[1024]{0:T(1024)}, u32[]{:S(2)}) copy-start(s32[1024]{0:T(1024)} %param.17) | copy-start | bytes 12292
  133.2 20.9 %all-to-all-start.1 = ((bf16[4,2,160,512]{3,2,1,0:T(8,128)(2,1)}), bf16[4,2,160,512]{3,2,1,0:T(8,128)(2,1)S(1)}, u32[]{:S(2)}, u32[]{:S(2)}) async-start(bf16[4,2,160,512]{3,2,1,0:T(8,128)(2,1)} %copy.20), calls=%async_computation.1 | async-start | bytes 2621440 | tf_op jit(solution)/shard_map/all_to_all | solution.py:247
  154.2 1.2 copy-start.4
Sparse Core Ops, SparseCore 0:
  8.9 47.5 all-gather.2
where the time goes:
time: 167 us; the launch traced here: 165 us
  blocking collectives  51.4 us (31%)
  waiting for transfers between devices  32.7 us (20%)
  matrix products  29.4 us (18%)
  Pallas kernels  24 us (14%)
  between operations  13.5 us (8%)
  local copies, waits for them, and re-layouts  8.37 us (5%)
  starting transfers between devices  4.54 us (3%)
    dot_general x1, matrix products, run_experts(): jnp.einsum('secf,efd->secd', inner, second_weight, preferred_element_type...  27.6 us
    pallas_call x1, Pallas kernels, attention(): pl.pallas_call(attention_kernel, grid=(rows // WTOK,), out_shape=(jax.Sha...  20.9 us
    all_gather x1, blocking collectives, shards(): wproj = lax.all_gather(proj_weight, 'fsdp', axis=0, tiled=True)  20.3 us
    all_to_all x1, blocking collectives, shards(): lax.all_to_all(packed.reshape(ranks, held, cap, width), 'expert', split_a...  19.5 us
    all_to_all x1, waiting for transfers between devices, shards(): lax.all_to_all(answers, 'expert', split_axis=0, concat_axis=0, tiled=True)  16.2 us
    all_gather x1, waiting for transfers between devices, shards(): wqkv = lax.all_gather(qkv_weight, 'fsdp', axis=0, tiled=True)  15.7 us
    all_gather x1, blocking collectives, shards(): net = lax.all_gather(net, 'fsdp', axis=0)  11.6 us
    unnamed x25, local copies, waits for them, and re-layouts  7.09 us
  transfers between devices with their start and end apart: 2, of which 2 were waited for; matrix products, arithmetic and copies ran while one was open for 1% of the time, Pallas kernels for 0%

commit v1 on v0

--- a/solution.py
+++ b/solution.py
@@ -212,10 +212,320 @@
     )(residual, normed, router, routes.reshape(1, rows), slot_ids.reshape(1, rows), returned)
 
 
-def run_experts(arrived, first_weight, second_weight):
-    inner = jnp.einsum("secd,edf->secf", arrived, first_weight, preferred_element_type=F32)
-    inner = jax.nn.gelu(inner, approximate=False).astype(BF16)
-    return jnp.einsum("secf,efd->secd", inner, second_weight, preferred_element_type=F32).astype(BF16)
+MESH = pl.DeviceIdType.MESH
+
+
+def gather_kernel(shards_total, *refs):
+    wqkv_ref, wproj_ref, net_ref, qkv_out, proj_out, net_out = refs[:6]
+    up_send, up_recv, down_send, down_recv, sib_send, sib_recv, local = refs[6:]
+    me = lax.axis_index("fsdp")
+    rank = lax.axis_index("expert")
+    core = lax.rem(rank, 2)
+    sibling = {"expert": rank + 1 - 2 * core}
+    above, below = {"fsdp": me + 1}, {"fsdp": me - 1}
+    has_above, has_below = me + 1 < shards_total, me >= 1
+    rows = wqkv_ref.shape[0]
+    half = rows // 2
+    width = wproj_ref.shape[1]
+
+    barrier = pltpu.get_barrier_semaphore()
+
+    @pl.when(has_above)
+    def _():
+        pl.semaphore_signal(barrier, inc=1, device_id=above, device_id_type=MESH)
+
+    @pl.when(has_below)
+    def _():
+        pl.semaphore_signal(barrier, inc=1, device_id=below, device_id_type=MESH)
+
+    pl.semaphore_signal(barrier, inc=1, device_id=sibling, device_id_type=MESH)
+
+    peers = 1 + has_above.astype(jnp.int32) + has_below.astype(jnp.int32)
+    pl.semaphore_wait(barrier, peers)
+
+    pieces = ["net"]
+    for c in range(wqkv_ref.shape[1] // width):
+        pieces.append((wqkv_ref, qkv_out, c * width))
+    pieces.append((wproj_ref, proj_out, 0))
+
+    def place(piece, shard, part):
+        if piece == "net":
+            return net_out.at[shard]
+        _, out, col = piece
+        start = pl.multiple_of(shard * rows + part * half, half)
+        return out.at[pl.ds(start, half), pl.ds(col, width)]
+
+    def own(piece):
+        if piece == "net":
+            return net_ref
+        ref, _, col = piece
+        return ref.at[pl.ds(pl.multiple_of(core * half, half), half), pl.ds(col, width)]
+
+    def hop(piece, p, step, shard, upward):
+        send, recv = (up_send, up_recv) if upward else (down_send, down_recv)
+        target = place(piece, shard, core)
+        return pltpu.make_async_remote_copy(
+            src_ref=own(piece) if step == 0 else target,
+            dst_ref=target,
+            send_sem=send.at[step, p],
+            recv_sem=recv.at[step, p],
+            device_id=above if upward else below,
+            device_id_type=MESH,
+        )
+
+    def aside(piece, p, slot, shard, part):
+        block = place(piece, shard, part)
+        return pltpu.make_async_remote_copy(
+            src_ref=block,
+            dst_ref=block,
+            send_sem=sib_send.at[slot, p],
+            recv_sem=sib_recv.at[slot, p],
+            device_id=sibling,
+            device_id_type=MESH,
+        )
+
+    locals_ = [
+        pltpu.make_async_copy(
+            wqkv_ref, qkv_out.at[pl.ds(pl.multiple_of(me * rows, rows), rows)], local.at[0]
+        ),
+        pltpu.make_async_copy(
+            wproj_ref, proj_out.at[pl.ds(pl.multiple_of(me * rows, rows), rows)], local.at[1]
+        ),
+        pltpu.make_async_copy(net_ref, net_out.at[me], local.at[2]),
+    ]
+    steps = shards_total - 1
+    for step in range(steps + 1):
+        for p, piece in enumerate(pieces):
+            for upward in (True, False):
+                sign = -1 if upward else 1
+                shard = me + sign * step
+                held = (shard >= 0) if upward else (shard < shards_total)
+                further = has_above if upward else has_below
+                if step > 0:
+                    slot = (step - 1) * 2 + (0 if upward else 1)
+
+                    @pl.when(held)
+                    def _():
+                        hop(piece, p, step - 1, shard, upward).wait_recv()
+                        if piece != "net":
+                            aside(piece, p, slot, shard, core).start()
+
+                if step < steps:
+
+                    @pl.when(held & further)
+                    def _():
+                        hop(piece, p, step, shard, upward).start()
+
+        if step == 0:
+            for copy in locals_:
+                copy.start()
+    for step in range(steps + 1):
+        for p, piece in enumerate(pieces):
+            for upward in (True, False):
+                sign = -1 if upward else 1
+                shard = me + sign * step
+                held = (shard >= 0) if upward else (shard < shards_total)
+                further = has_above if upward else has_below
+                if step > 0 and piece != "net":
+                    slot = (step - 1) * 2 + (0 if upward else 1)
+
+                    @pl.when(held)
+                    def _():
+                        aside(piece, p, slot, shard, core).wait_send()
+                        aside(piece, p, slot, shard, 1 - core).wait_recv()
+
+                if step < steps:
+
+                    @pl.when(held & further)
+                    def _():
+                        hop(piece, p, step, shard, upward).wait_send()
+
+    for copy in locals_:
+        copy.wait()
+
+
+def gather_weights(qkv_weight, proj_weight, net):
+    total = lax.axis_size("fsdp")
+    rows, width = proj_weight.shape
+    pieces = qkv_weight.shape[1] // width + 2
+    anywhere = pl.BlockSpec(memory_space=pl.ANY)
+    dma = pltpu.SemaphoreType.DMA
+    return pl.pallas_call(
+        functools.partial(gather_kernel, total),
+        out_shape=(
+            jax.ShapeDtypeStruct((total * rows, qkv_weight.shape[1]), BF16),
+            jax.ShapeDtypeStruct((total * rows, width), BF16),
+            jax.ShapeDtypeStruct((total,) + net.shape, F32),
+        ),
+        in_specs=[anywhere] * 3,
+        out_specs=(anywhere,) * 3,
+        scratch_shapes=[dma((total - 1, pieces)) for _ in range(4)]
+        + [dma((2 * (total - 1), pieces)) for _ in range(2)]
+        + [dma((3,))],
+        compiler_params=pltpu.CompilerParams(collective_id=0, has_side_effects=True),
+        name="gather_weights",
+    )(qkv_weight, proj_weight, net)
+
+
+def expert_kernel(chips, held, capp, *refs):
+    normed_ref, routes_ref, slots_ref, win_any, wout_any, ret_ref = refs[:6]
+    packed, arrived, answers, win, wout = refs[6:11]
+    load, out_send, out_recv, back_send, back_recv, keep = refs[11:]
+    rank = lax.axis_index("expert")
+    chip, core = rank // 2, lax.rem(rank, 2)
+
+    def rank_of(offset, which):
+        return lax.rem(chip + offset, chips) * 2 + which
+
+    barrier = pltpu.get_barrier_semaphore()
+    for offset in range(1, 2 * chips):
+        other = lax.rem(rank + offset, 2 * chips)
+        pl.semaphore_signal(barrier, inc=1, device_id={"expert": other}, device_id_type=MESH)
+
+    loads = []
+    for e in range(held):
+        loads.append(
+            (
+                pltpu.make_async_copy(win_any.at[e], win.at[e], load.at[2 * e]),
+                pltpu.make_async_copy(wout_any.at[e], wout.at[e], load.at[2 * e + 1]),
+            )
+        )
+        loads[e][0].start()
+        loads[e][1].start()
+
+    tokens = normed_ref.shape[0]
+    spot = lax.broadcasted_iota(jnp.int32, (capp, tokens), 0)
+
+    def pack(expert):
+        hit = (spot == slots_ref[...]) & (routes_ref[...] == expert)
+        return dot(jnp.where(hit, 1.0, 0.0).astype(BF16), normed_ref[...]).astype(BF16)
+
+    def spread(k, which, e):
+        far = (chips - k) % chips
+        target = rank_of(k, which)
+        return pltpu.make_async_remote_copy(
+            src_ref=packed.at[target * held + e],
+            dst_ref=arrived.at[far, e, core],
+            send_sem=out_send.at[k, which, e],
+            recv_sem=out_recv.at[far, core, e],
+            device_id={"expert": target},
+            device_id_type=MESH,
+        )
+
+    def spread_arrival(k, which, e):
+        target = rank_of(k, which)
+        return pltpu.make_async_remote_copy(
+            src_ref=packed.at[target * held + e],
+            dst_ref=arrived.at[k, e, which],
+            send_sem=out_send.at[k, which, e],
+            recv_sem=out_recv.at[k, which, e],
+            device_id={"expert": target},
+            device_id_type=MESH,
+        )
+
+    def back(k, which, e):
+        target = rank_of(k, which)
+        return pltpu.make_async_remote_copy(
+            src_ref=answers.at[k, e, which],
+            dst_ref=ret_ref.at[rank * held + e],
+            send_sem=back_send.at[k, which, e],
+            recv_sem=back_recv.at[(chips - k) % chips, core, e],
+            device_id={"expert": target},
+            device_id_type=MESH,
+        )
+
+    def back_arrival(k, which, e):
+        target = rank_of(k, which)
+        return pltpu.make_async_remote_copy(
+            src_ref=answers.at[k, e, which],
+            dst_ref=ret_ref.at[target * held + e],
+            send_sem=back_send.at[k, which, e],
+            recv_sem=back_recv.at[k, which, e],
+            device_id={"expert": target},
+            device_id_type=MESH,
+        )
+
+    def partners(k):
+        return (0, 1) if k else (1 - core,)
+
+    first = True
+    for k in list(range(1, chips)) + [0]:
+        for e in range(held):
+            for which in partners(k):
+                expert = rank_of(k, which) * held + e
+                packed[expert] = pack(expert)
+                if first:
+                    pl.semaphore_wait(barrier, 2 * chips - 1)
+                    first = False
+                spread(k, which, e).start()
+    for e in range(held):
+        arrived[0, e, core] = pack(rank * held + e)
+
+    ff = win.shape[2]
+    chunk = 512
+    for k in range(chips):
+        for e in range(held):
+            if k == 0:
+                loads[e][0].wait()
+                loads[e][1].wait()
+            for which in partners(k):
+                spread_arrival(k, which, e).wait_recv()
+            x = arrived[k, e].reshape(2 * capp, arrived.shape[-1])
+            total = None
+            for f in range(0, ff, chunk):
+                inner = dot(x, win[e, :, f : f + chunk])
+                inner = (0.5 * inner * (1.0 + lax.erf(inner * math.sqrt(0.5)))).astype(BF16)
+                part = dot(inner, wout[e, f : f + chunk, :])
+                total = part if total is None else total + part
+            answers[k, e] = total.astype(BF16).reshape(2, capp, arrived.shape[-1])
+            for which in partners(k):
+                back(k, which, e).start()
+            if k == 0:
+                pltpu.make_async_copy(
+                    answers.at[0, e, core], ret_ref.at[rank * held + e], keep.at[e]
+                ).start()
+    for k in range(chips):
+        for e in range(held):
+            for which in partners(k):
+                spread(k, which, e).wait_send()
+                back(k, which, e).wait_send()
+                back_arrival(k, which, e).wait_recv()
+    for e in range(held):
+        pltpu.make_async_copy(
+            answers.at[0, e, core], ret_ref.at[rank * held + e], keep.at[e]
+        ).wait()
+
+
+def run_experts(normed, routes, slot_ids, expert_in, expert_out, experts, capp):
+    rows, width = normed.shape
+    held, _, ff = expert_in.shape
+    chips = lax.axis_size("expert") // 2
+    anywhere = pl.BlockSpec(memory_space=pl.ANY)
+    near = pl.BlockSpec(memory_space=pltpu.VMEM)
+    dma = pltpu.SemaphoreType.DMA
+    return pl.pallas_call(
+        functools.partial(expert_kernel, chips, held, capp),
+        out_shape=jax.ShapeDtypeStruct((experts, capp, width), BF16),
+        in_specs=[near, near, near, anywhere, anywhere],
+        out_specs=anywhere,
+        scratch_shapes=[
+            pltpu.VMEM((experts, capp, width), BF16),
+            pltpu.VMEM((chips, held, 2, capp, width), BF16),
+            pltpu.VMEM((chips, held, 2, capp, width), BF16),
+            pltpu.VMEM((held, width, ff), BF16),
+            pltpu.VMEM((held, ff, width), BF16),
+            dma((2 * held,)),
+            dma((chips, 2, held)),
+            dma((chips, 2, held)),
+            dma((chips, 2, held)),
+            dma((chips, 2, held)),
+            dma((held,)),
+        ],
+        compiler_params=pltpu.CompilerParams(
+            collective_id=1, has_side_effects=True, vmem_limit_bytes=48 * MIB
+        ),
+        name="experts",
+    )(normed, routes.reshape(1, rows), slot_ids.reshape(1, rows), expert_in, expert_out)
 
 
 def shards(
@@ -227,26 +537,14 @@
     net = jnp.concatenate(
         [second_weight.T, first_weight, first_offset[None], jnp.zeros((5, units), F32)], axis=0
     )
-    net = lax.all_gather(net, "fsdp", axis=0)
-    wqkv = lax.all_gather(qkv_weight, "fsdp", axis=0, tiled=True)
-    wproj = lax.all_gather(proj_weight, "fsdp", axis=0, tiled=True)
+    wqkv, wproj, net = gather_weights(qkv_weight, proj_weight, net)
     residual, normed = attention(tokens, wqkv, wproj, net, logit_scale, attn_gain, moe_gain)
     experts = router.shape[1]
-    held = expert_in.shape[0]
-    ranks = lax.axis_size("expert")
     cap = rows * 5 // (4 * experts)
-    column = routes * cap + slot_ids
-    one_hot = (column[:, None] == jnp.arange(experts * cap, dtype=jnp.int32)[None, :]).astype(BF16)
-    packed = lax.dot_general(
-        one_hot, normed, (((0,), (0,)), ((), ())), preferred_element_type=F32
-    ).astype(BF16)
-    arrived = lax.all_to_all(
-        packed.reshape(ranks, held, cap, width), "expert", split_axis=0, concat_axis=0, tiled=True
-    )
-    answers = run_experts(arrived, expert_in, expert_out)
-    returned = lax.all_to_all(answers, "expert", split_axis=0, concat_axis=0, tiled=True)
-    returned = returned.reshape(experts * cap, width)
-    return combine(residual, normed, router, routes, slot_ids, returned, cap)
+    capp = (cap + 15) // 16 * 16
+    returned = run_experts(normed, routes, slot_ids, expert_in, expert_out, experts, capp)
+    returned = returned.reshape(experts * capp, width)
+    return combine(residual, normed, router, routes, slot_ids, returned, capp)
 
 
 def solution(mesh):

time: 167 us -> 90.7 us (0.54)
  Pallas kernels: 24 us -> 80.3 us
  blocking collectives: 51.4 us -> 0 us
  waiting for transfers between devices: 32.7 us -> 0 us
  matrix products: 29.4 us -> 0 us
  between operations: 13.5 us -> 0.07 us
  starting transfers between devices: 4.54 us -> 0 us
    pallas_call x0 -> x2, Pallas kernels: none -> 56.3 us  [the longest x1 31 us: run_experts(): pl.pallas_call(functools.partial(expert_kernel, chips, held, capp), out_s...]
    all_gather x2 -> x0, blocking collectives: 31.9 us -> none  [the longest x1 20.3 us: shards(): wproj = lax.all_gather(proj_weight, 'fsdp', axis=0, tiled=True)]
    dot_general x2 -> x0, matrix products: 29.4 us -> none  [the longest x1 27.6 us: run_experts(): jnp.einsum('secf,efd->secd', inner, second_weight, preferred_element_type...]
    all_to_all x1 -> x0, blocking collectives: 19.5 us -> none  [shards(): lax.all_to_all(packed.reshape(ranks, held, cap, width), 'expert', split_a...]
    all_to_all x1 -> x0, waiting for transfers between devices: 16.2 us -> none  [shards(): lax.all_to_all(answers, 'expert', split_axis=0, concat_axis=0, tiled=True)]
    all_gather x1 -> x0, waiting for transfers between devices: 15.7 us -> none  [shards(): wqkv = lax.all_gather(qkv_weight, 'fsdp', axis=0, tiled=True)]
    all_to_all x1 -> x0, starting transfers between devices: 4.54 us -> none  [shards(): lax.all_to_all(answers, 'expert', split_axis=0, concat_axis=0, tiled=True)]
    unnamed x25 -> x23, local copies, waits for them, and re-layouts: 7.09 us -> 8.39 us
  transfers between devices with their start and end apart: 2 -> 0, of which waited for: 2 -> 0; matrix products, arithmetic and copies ran while one was open for 1% -> 0% of each run, Pallas kernels for 0% -> 0%
where the time goes in v1:
time: 90.7 us; the launch traced here: 90.2 us
  Pallas kernels  80.3 us (89%)
  local copies, waits for them, and re-layouts  8.47 us (9%)
  other arithmetic  1.4 us (2%)
    pallas_call x1, Pallas kernels, run_experts(): pl.pallas_call(functools.partial(expert_kernel, chips, held, capp), out_s...  31 us
    pallas_call x1, Pallas kernels, gather_weights(): pl.pallas_call(functools.partial(gather_kernel, total), out_shape=(jax.Sh...  25.3 us
    pallas_call x1, Pallas kernels, attention(): pl.pallas_call(attention_kernel, grid=(rows // WTOK,), out_shape=(jax.Sha...  20.8 us
    unnamed x23, local copies, waits for them, and re-layouts  8.39 us
    pallas_call x1, Pallas kernels, combine(): pl.pallas_call(functools.partial(combine_kernel, cap), grid=(rows // step...  3.14 us

profile of v1, /device:TPU:1, one launch (start us, length us, event | category | flops | bytes accessed | tf_op | source)
XLA Modules:
  0.0 90.2 jit_solution(5854396198690167804)
XLA Ops:
  0.0 0.1 pad.3.clone
  0.1 1.4 %maximum_maximum_fusion.refs_2_ = f32[24,128]{1,0:T(8,128)} fusion(f32[1,128]{1,0:T(1,128)} %bitcast.17, f32[2,128]{1,0:T(2,128)} %param.21, f32[16,128]{1,0:T(8,128)} %bitcast.16, f32[24]{0:T(128)S(1)} %pad.3.clone), kind=kLoop, calls=%fused_computation | loop fusion | flops 9216 | bytes 22112 | tf_op jit(solution)/shard_map/concatenate | solution.py:537
  1.5 0.9 copy.16.router_ref
  2.3 0.0 copy-start.6
  2.4 0.0 copy-start.7
  2.4 25.3 %gather_weights.1 = (bf16[512,1536]{1,0:T(8,128)(2,1)}, bf16[512,512]{1,0:T(8,128)(2,1)}, f32[4,24,128]{2,1,0:T(8,128)}) custom-call(bf16[128,1536]{1,0:T(8,128)(2,1)} %refs_0_.1, bf16[128,512]{1,0:T(8,128)(2,1)} %refs_1_.1, f32[24,128]{1,0:T(8,128)} %maximum_maximum_fusion.refs_2_), custom_call_target="tpu_custom_call" | custom-call | tf_op jit(solution)/shard_map/gather_weights/pallas_call | solution.py:353
  27.7 0.0 copy-start.1
  27.7 1.4 %copy-done.1 = bf16[512,1536]{1,0:T(8,128)(2,1)S(1)} copy-done((bf16[512,1536]{1,0:T(8,128)(2,1)S(1)}, bf16[512,1536]{1,0:T(8,128)(2,1)}, u32[]{:S(2)}) %copy-start.1) | copy-done | bytes 1572888
  29.1 0.0 copy-start.2
  29.1 1.2 %copy-done.2 = bf16[1024,512]{1,0:T(8,128)(2,1)S(1)} copy-done((bf16[1024,512]{1,0:T(8,128)(2,1)S(1)}, bf16[1024,512]{1,0:T(8,128)(2,1)}, u32[]{:S(2)}) %copy-start.2) | copy-done | bytes 1048600
  30.3 0.0 copy-start.3
  30.3 1.0 %copy-done.3 = f32[1024,8]{1,0:T(8,128)S(1)} copy-done((f32[1024,8]{1,0:T(8,128)S(1)}, f32[1024,8]{1,0:T(8,128)}, u32[]{:S(2)}) %copy-start.3) | copy-done | bytes 32792
  31.4 0.0 copy-start.4
  31.4 1.0 %copy-done.4 = bf16[512,512]{1,0:T(8,128)(2,1)S(1)} copy-done((bf16[512,512]{1,0:T(8,128)(2,1)S(1)}, bf16[512,512]{1,0:T(8,128)(2,1)}, u32[]{:S(2)}) %copy-start.4) | copy-done | bytes 524312
  32.4 0.8 copy-done.5
  33.2 0.7 copy-done.8
  33.9 0.7 copy-done.9
  34.6 0.7 copy-done.10
  35.2 20.8 %attention.1 = (f32[1024,512]{1,0:T(8,128)}, bf16[1024,512]{1,0:T(8,128)(2,1)S(1)}) custom-call(bf16[1024,512]{1,0:T(8,128)(2,1)S(1)} %copy-done.2, bf16[512,1536]{1,0:T(8,128)(2,1)S(1)} %copy-done.1, bf16[512,512]{1,0:T(8,128)(2,1)S(1)} %copy-done.4, f32[4,24,128]{2,1,0:T(8,128)S(1)} %copy-done.5, f32[1024,8]{1,0:T(8,128)S(1)} %copy-done.3, ...), custom_call_target="tpu_custom_call" | custom-call | tf_op jit(solution)/shard_map/attention/pallas_call | solution.py:142
  56.1 0.0 copy-done.6
  56.1 0.0 copy-done.7
  56.1 31.0 %experts.1 = bf16[8,160,512]{2,1,0:T(8,128)(2,1)S(1)} custom-call(bf16[1024,512]{1,0:T(8,128)(2,1)S(1)} %get-tuple-element.14.refs_0_.normed_ref, s32[1,1024]{1,0:T(1,128)S(1)} %bitcast.9, s32[1,1024]{1,0:T(1,128)S(1)} %bitcast.11, bf16[2,512,2048]{2,1,0:T(8,128)(2,1)} %refs_3_.1, bf16[2,2048,512]{2,1,0:T(8,128)(2,1)} %refs_4_.1), custom_call_target="tpu_custom_call" | custom-call | tf_op jit(solution)/shard_map/experts/pallas_call | solution.py:506
  87.1 0.0 copy-done
  87.1 3.1 %combine.1 = bf16[1024,512]{1,0:T(8,128)(2,1)} custom-call(f32[1024,512]{1,0:T(8,128)S(1)} %copy-done, bf16[1024,512]{1,0:T(8,128)(2,1)S(1)} %get-tuple-element.14.refs_0_.normed_ref, bf16[512,8]{1,0:T(8,128)(2,1)S(1)} %copy.16.router_ref, s32[1,1024]{1,0:T(1,128)S(1)} %bitcast.10, s32[1,1024]{1,0:T(1,128)S(1)} %bitcast.12, bf16[1280,512]{1,0:T(8,128)(2,1)S(1)} %bitcast.8), custom_call_target="tpu_custom_call" | custom-call | tf_op jit(solution)/shard_map/combine/pallas_call | solution.py:201
  (6 shorter events, 0.0 us)
Async XLA Ops:
  2.3 53.7 %copy-start.6 = (s32[1024]{0:T(1024)S(1)}, s32[1024]{0:T(1024)}, u32[]{:S(2)}) copy-start(s32[1024]{0:T(1024)} %param.16) | copy-start | bytes 12292
  2.4 53.7 %copy-start.7 = (s32[1024]{0:T(1024)S(1)}, s32[1024]{0:T(1024)}, u32[]{:S(2)}) copy-start(s32[1024]{0:T(1024)} %param.17) | copy-start | bytes 12292
  27.7 1.4 %copy-start.1 = (bf16[512,1536]{1,0:T(8,128)(2,1)S(1)}, bf16[512,1536]{1,0:T(8,128)(2,1)}, u32[]{:S(2)}) copy-start(bf16[512,1536]{1,0:T(8,128)(2,1)} %get-tuple-element.10.wqkv_ref) | copy-start | bytes 4718596
  29.1 1.2 %copy-start.2 = (bf16[1024,512]{1,0:T(8,128)(2,1)S(1)}, bf16[1024,512]{1,0:T(8,128)(2,1)}, u32[]{:S(2)}) copy-start(bf16[1024,512]{1,0:T(8,128)(2,1)} %tok_ref.1) | copy-start | bytes 3145732
  30.3 1.0 %copy-start.3 = (f32[1024,8]{1,0:T(8,128)S(1)}, f32[1024,8]{1,0:T(8,128)}, u32[]{:S(2)}) copy-start(f32[1024,8]{1,0:T(8,128)} %constant.4.clone.coords_ref) | copy-start | bytes 98308
  31.4 1.0 %copy-start.4 = (bf16[512,512]{1,0:T(8,128)(2,1)S(1)}, bf16[512,512]{1,0:T(8,128)(2,1)}, u32[]{:S(2)}) copy-start(bf16[512,512]{1,0:T(8,128)(2,1)} %get-tuple-element.11.wproj_ref) | copy-start | bytes 1572868
  32.4 0.8 copy-start.5
  33.2 0.7 copy-start.8
  33.9 0.7 copy-start.9
  34.6 0.7 copy-start.10
  56.1 31.0 %copy-start = (f32[1024,512]{1,0:T(8,128)S(1)}, f32[1024,512]{1,0:T(8,128)}, u32[]{:S(2)}) copy-start(f32[1024,512]{1,0:T(8,128)} %get-tuple-element.13.res_ref) | copy-start | bytes 6291460

commit v2 on v1

--- a/solution.py
+++ b/solution.py
@@ -163,7 +163,7 @@
             pltpu.VMEM((256, 256), BF16),
             pltpu.VMEM((WTOK, width), BF16),
         ],
-        compiler_params=pltpu.CompilerParams(vmem_limit_bytes=48 * MIB),
+        compiler_params=pltpu.CompilerParams(vmem_limit_bytes=60 * MIB),
         name="attention",
     )(
         tokens, wqkv, wproj, net, coords, logit_scale.reshape(1, HEADS),
@@ -207,7 +207,7 @@
             whole_block(returned.shape),
         ],
         out_specs=rows_block,
-        compiler_params=pltpu.CompilerParams(vmem_limit_bytes=48 * MIB),
+        compiler_params=pltpu.CompilerParams(vmem_limit_bytes=60 * MIB),
         name="combine",
     )(residual, normed, router, routes.reshape(1, rows), slot_ids.reshape(1, rows), returned)
 
@@ -217,16 +217,19 @@
 
 def gather_kernel(shards_total, *refs):
     wqkv_ref, wproj_ref, net_ref, qkv_out, proj_out, net_out = refs[:6]
-    up_send, up_recv, down_send, down_recv, sib_send, sib_recv, local = refs[6:]
+    up_send, up_recv, down_send, down_recv = refs[6:10]
+    sib_send, sib_recv, far_send, far_recv, on_send, on_recv, local = refs[10:]
     me = lax.axis_index("fsdp")
     rank = lax.axis_index("expert")
     core = lax.rem(rank, 2)
+    side = lax.rem(rank // 2, 2)
+    mine, theirs = side * 2 + core, (1 - side) * 2 + core
     sibling = {"expert": rank + 1 - 2 * core}
+    across = {"expert": rank + 2 - 4 * side}
     above, below = {"fsdp": me + 1}, {"fsdp": me - 1}
     has_above, has_below = me + 1 < shards_total, me >= 1
     rows = wqkv_ref.shape[0]
-    half = rows // 2
-    width = wproj_ref.shape[1]
+    quarter = rows // 4
 
     barrier = pltpu.get_barrier_semaphore()
 
@@ -239,31 +242,27 @@
         pl.semaphore_signal(barrier, inc=1, device_id=below, device_id_type=MESH)
 
     pl.semaphore_signal(barrier, inc=1, device_id=sibling, device_id_type=MESH)
-
-    peers = 1 + has_above.astype(jnp.int32) + has_below.astype(jnp.int32)
+    pl.semaphore_signal(barrier, inc=1, device_id=across, device_id_type=MESH)
+
+    peers = 2 + has_above.astype(jnp.int32) + has_below.astype(jnp.int32)
     pl.semaphore_wait(barrier, peers)
 
-    pieces = ["net"]
-    for c in range(wqkv_ref.shape[1] // width):
-        pieces.append((wqkv_ref, qkv_out, c * width))
-    pieces.append((wproj_ref, proj_out, 0))
+    pieces = ["net", (wqkv_ref, qkv_out), (wproj_ref, proj_out)]
 
     def place(piece, shard, part):
         if piece == "net":
             return net_out.at[shard]
-        _, out, col = piece
-        start = pl.multiple_of(shard * rows + part * half, half)
-        return out.at[pl.ds(start, half), pl.ds(col, width)]
+        start = pl.multiple_of(shard * rows + part * quarter, quarter)
+        return piece[1].at[pl.ds(start, quarter)]
 
     def own(piece):
         if piece == "net":
             return net_ref
-        ref, _, col = piece
-        return ref.at[pl.ds(pl.multiple_of(core * half, half), half), pl.ds(col, width)]
+        return piece[0].at[pl.ds(pl.multiple_of(mine * quarter, quarter), quarter)]
 
     def hop(piece, p, step, shard, upward):
         send, recv = (up_send, up_recv) if upward else (down_send, down_recv)
-        target = place(piece, shard, core)
+        target = place(piece, shard, mine)
         return pltpu.make_async_remote_copy(
             src_ref=own(piece) if step == 0 else target,
             dst_ref=target,
@@ -273,16 +272,29 @@
             device_id_type=MESH,
         )
 
-    def aside(piece, p, slot, shard, part):
+    def push(piece, p, slot, shard, part, sems, device):
         block = place(piece, shard, part)
         return pltpu.make_async_remote_copy(
             src_ref=block,
             dst_ref=block,
-            send_sem=sib_send.at[slot, p],
-            recv_sem=sib_recv.at[slot, p],
-            device_id=sibling,
+            send_sem=sems[0].at[slot, p],
+            recv_sem=sems[1].at[slot, p],
+            device_id=device,
             device_id_type=MESH,
         )
+
+    near_sems, far_sems, on_sems = (sib_send, sib_recv), (far_send, far_recv), (on_send, on_recv)
+
+    def hand_on(step, p, piece):
+        for upward in (True, False):
+            shard = me - step if upward else me + step
+            held = (shard >= 0) if upward else (shard < shards_total)
+            slot = (step - 1) * 2 + (0 if upward else 1)
+
+            @pl.when(held)
+            def _():
+                push(piece, p, slot, shard, theirs, far_sems, across).wait_recv()
+                push(piece, p, slot, shard, theirs, on_sems, sibling).start()
 
     locals_ = [
         pltpu.make_async_copy(
@@ -308,7 +320,8 @@
                     def _():
                         hop(piece, p, step - 1, shard, upward).wait_recv()
                         if piece != "net":
-                            aside(piece, p, slot, shard, core).start()
+                            push(piece, p, slot, shard, mine, far_sems, across).start()
+                            push(piece, p, slot, shard, mine, near_sems, sibling).start()
 
                 if step < steps:
 
@@ -316,9 +329,15 @@
                     def _():
                         hop(piece, p, step, shard, upward).start()
 
+            if step > 1 and piece != "net":
+                hand_on(step - 1, p, piece)
+
         if step == 0:
             for copy in locals_:
                 copy.start()
+    for p, piece in enumerate(pieces):
+        if piece != "net":
+            hand_on(steps, p, piece)
     for step in range(steps + 1):
         for p, piece in enumerate(pieces):
             for upward in (True, False):
@@ -331,8 +350,13 @@
 
                     @pl.when(held)
                     def _():
-                        aside(piece, p, slot, shard, core).wait_send()
-                        aside(piece, p, slot, shard, 1 - core).wait_recv()
+                        beside = side * 2 + 1 - core
+                        push(piece, p, slot, shard, mine, far_sems, across).wait_send()
+                        push(piece, p, slot, shard, mine, near_sems, sibling).wait_send()
+                        push(piece, p, slot, shard, theirs, on_sems, sibling).wait_send()
+                        push(piece, p, slot, shard, beside, near_sems, sibling).wait_recv()
+                        crossed = (1 - side) * 2 + 1 - core
+                        push(piece, p, slot, shard, crossed, on_sems, sibling).wait_recv()
 
                 if step < steps:
 
@@ -347,7 +371,7 @@
 def gather_weights(qkv_weight, proj_weight, net):
     total = lax.axis_size("fsdp")
     rows, width = proj_weight.shape
-    pieces = qkv_weight.shape[1] // width + 2
+    pieces = 3
     anywhere = pl.BlockSpec(memory_space=pl.ANY)
     dma = pltpu.SemaphoreType.DMA
     return pl.pallas_call(
@@ -360,7 +384,7 @@
         in_specs=[anywhere] * 3,
         out_specs=(anywhere,) * 3,
         scratch_shapes=[dma((total - 1, pieces)) for _ in range(4)]
-        + [dma((2 * (total - 1), pieces)) for _ in range(2)]
+        + [dma((2 * (total - 1), pieces)) for _ in range(6)]
         + [dma((3,))],
         compiler_params=pltpu.CompilerParams(collective_id=0, has_side_effects=True),
         name="gather_weights",
@@ -522,7 +546,7 @@
             dma((held,)),
         ],
         compiler_params=pltpu.CompilerParams(
-            collective_id=1, has_side_effects=True, vmem_limit_bytes=48 * MIB
+            collective_id=1, has_side_effects=True, vmem_limit_bytes=60 * MIB
         ),
         name="experts",
     )(normed, routes.reshape(1, rows), slot_ids.reshape(1, rows), expert_in, expert_out)

time: 90.7 us -> 87.6 us (0.966)
  local copies, waits for them, and re-layouts: 8.47 us -> 1.55 us
  Pallas kernels: 80.3 us -> 84.3 us
    unnamed x23 -> x1, local copies, waits for them, and re-layouts: 8.39 us -> 1.47 us
    pallas_call x1, Pallas kernels: 3.14 us -> 5.53 us  [combine(): pl.pallas_call(functools.partial(combine_kernel, cap), grid=(rows // step...]
    pallas_call x1, Pallas kernels: 20.8 us -> 22.9 us  [attention(): pl.pallas_call(attention_kernel, grid=(rows // WTOK,), out_shape=(jax.Sha...]
    pallas_call x1, Pallas kernels: 25.3 us -> 23.6 us  [gather_weights(): pl.pallas_call(functools.partial(gather_kernel, total), out_shape=(jax.Sh...]
    pallas_call x1, Pallas kernels: 31 us -> 32.3 us  [run_experts(): pl.pallas_call(functools.partial(expert_kernel, chips, held, capp), out_s...]
where the time goes in v2:
time: 87.6 us; the launch traced here: 87.3 us
  Pallas kernels  84.3 us (96%)
  local copies, waits for them, and re-layouts  1.55 us (2%)
  other arithmetic  1.4 us (2%)
    pallas_call x1, Pallas kernels, run_experts(): pl.pallas_call(functools.partial(expert_kernel, chips, held, capp), out_s...  32.3 us
    pallas_call x1, Pallas kernels, gather_weights(): pl.pallas_call(functools.partial(gather_kernel, total), out_shape=(jax.Sh...  23.6 us
    pallas_call x1, Pallas kernels, attention(): pl.pallas_call(attention_kernel, grid=(rows // WTOK,), out_shape=(jax.Sha...  22.9 us
    pallas_call x1, Pallas kernels, combine(): pl.pallas_call(functools.partial(combine_kernel, cap), grid=(rows // step...  5.53 us

profile of v2, /device:TPU:1, one launch (start us, length us, event | category | flops | bytes accessed | tf_op | source)
XLA Modules:
  0.0 87.3 jit_solution(11486594327562415171)
XLA Ops:
  0.0 0.1 pad.3.clone
  0.1 1.4 %maximum_maximum_fusion.refs_2_ = f32[24,128]{1,0:T(8,128)} fusion(f32[1,128]{1,0:T(1,128)} %bitcast.17, f32[2,128]{1,0:T(2,128)} %param.21, f32[16,128]{1,0:T(8,128)} %bitcast.13, f32[24]{0:T(128)S(1)} %pad.3.clone), kind=kLoop, calls=%fused_computation | loop fusion | flops 9216 | bytes 22112 | tf_op jit(solution)/shard_map/concatenate | solution.py:561
  1.5 1.5 %copy.16.router_ref = bf16[512,8]{1,0:T(8,128)(2,1)} copy(bf16[512,8]{0,1:T(8,128)(2,1)} %param.25) | data formatting | bytes 16384 | tf_op args[10]
  3.0 23.6 %gather_weights.1 = (bf16[512,1536]{1,0:T(8,128)(2,1)}, bf16[512,512]{1,0:T(8,128)(2,1)}, f32[4,24,128]{2,1,0:T(8,128)}) custom-call(bf16[128,1536]{1,0:T(8,128)(2,1)} %refs_0_.1, bf16[128,512]{1,0:T(8,128)(2,1)} %refs_1_.1, f32[24,128]{1,0:T(8,128)} %maximum_maximum_fusion.refs_2_), custom_call_target="tpu_custom_call" | custom-call | tf_op jit(solution)/shard_map/gather_weights/pallas_call | solution.py:377
  26.6 22.9 %attention.1 = (f32[1024,512]{1,0:T(8,128)}, bf16[1024,512]{1,0:T(8,128)(2,1)}) custom-call(bf16[1024,512]{1,0:T(8,128)(2,1)} %tok_ref.1, bf16[512,1536]{1,0:T(8,128)(2,1)} %get-tuple-element.10.wqkv_ref, bf16[512,512]{1,0:T(8,128)(2,1)} %get-tuple-element.11.wproj_ref, f32[4,24,128]{2,1,0:T(8,128)} %get-tuple-element.12.net_ref, ...), custom_call_target="tpu_custom_call" | custom-call | tf_op jit(solution)/shard_map/attention/pallas_call | solution.py:142
  49.5 32.3 %experts.1 = bf16[8,160,512]{2,1,0:T(8,128)(2,1)} custom-call(bf16[1024,512]{1,0:T(8,128)(2,1)} %get-tuple-element.14.refs_0_.normed_ref, s32[1,1024]{1,0:T(1,128)} %bitcast.9, s32[1,1024]{1,0:T(1,128)} %bitcast.11, bf16[2,512,2048]{2,1,0:T(8,128)(2,1)} %refs_3_.1, bf16[2,2048,512]{2,1,0:T(8,128)(2,1)} %refs_4_.1), custom_call_target="tpu_custom_call" | custom-call | tf_op jit(solution)/shard_map/experts/pallas_call | solution.py:530
  81.8 5.5 %combine.1 = bf16[1024,512]{1,0:T(8,128)(2,1)} custom-call(f32[1024,512]{1,0:T(8,128)} %get-tuple-element.13.res_ref, bf16[1024,512]{1,0:T(8,128)(2,1)} %get-tuple-element.14.refs_0_.normed_ref, bf16[512,8]{1,0:T(8,128)(2,1)} %copy.16.router_ref, s32[1,1024]{1,0:T(1,128)} %bitcast.10, s32[1,1024]{1,0:T(1,128)} %bitcast.12, bf16[1280,512]{1,0:T(8,128)(2,1)} %bitcast.8), custom_call_target="tpu_custom_call" | custom-call | tf_op jit(solution)/shard_map/combine/pallas_call | solution.py:201
  (1 shorter events, 0.0 us)

commit v3 on v2

--- a/solution.py
+++ b/solution.py
@@ -184,7 +184,7 @@
 
     routes = column(routes_ref[...])
     place = column(routes_ref[...] * cap + slots_ref[...])
-    logits = dot(normed_ref[...], router_ref[...])
+    logits = dot_nt(normed_ref[...], router_ref[...])
     expert = lax.broadcasted_iota(jnp.int32, logits.shape, 1)
     picked = jnp.sum(jnp.where(expert == routes, logits, 0.0), axis=1, keepdims=True)
     gate = jax.nn.sigmoid(picked)
@@ -207,7 +207,7 @@
             whole_block(returned.shape),
         ],
         out_specs=rows_block,
-        compiler_params=pltpu.CompilerParams(vmem_limit_bytes=60 * MIB),
+        compiler_params=pltpu.CompilerParams(vmem_limit_bytes=48 * MIB),
         name="combine",
     )(residual, normed, router, routes.reshape(1, rows), slot_ids.reshape(1, rows), returned)
 
@@ -568,7 +568,7 @@
     capp = (cap + 15) // 16 * 16
     returned = run_experts(normed, routes, slot_ids, expert_in, expert_out, experts, capp)
     returned = returned.reshape(experts * capp, width)
-    return combine(residual, normed, router, routes, slot_ids, returned, capp)
+    return combine(residual, normed, router.T, routes, slot_ids, returned, capp)
 
 
 def solution(mesh):

time: 87.6 us -> 85.2 us (0.973)
  Pallas kernels: 84.3 us -> 82.1 us
    pallas_call x1, Pallas kernels: 5.53 us -> 3.15 us  [combine(): pl.pallas_call(functools.partial(combine_kernel, cap), grid=(rows // step...]
where the time goes in v3:
time: 85.2 us; the launch traced here: 85 us
  Pallas kernels  82.1 us (96%)
  local copies, waits for them, and re-layouts  1.41 us (2%)
  other arithmetic  1.4 us (2%)
    pallas_call x1, Pallas kernels, run_experts(): pl.pallas_call(functools.partial(expert_kernel, chips, held, capp), out_s...  32.4 us
    pallas_call x1, Pallas kernels, gather_weights(): pl.pallas_call(functools.partial(gather_kernel, total), out_shape=(jax.Sh...  23.6 us
    pallas_call x1, Pallas kernels, attention(): pl.pallas_call(attention_kernel, grid=(rows // WTOK,), out_shape=(jax.Sha...  22.9 us
    pallas_call x1, Pallas kernels, combine(): pl.pallas_call(functools.partial(combine_kernel, cap), grid=(rows // step...  3.15 us

profile of v3, /device:TPU:1, one launch (start us, length us, event | category | flops | bytes accessed | tf_op | source)
XLA Modules:
  0.0 85.0 jit_solution(18342426985860351849)
XLA Ops:
  0.0 0.1 pad.3.clone
  0.1 1.4 %maximum_maximum_fusion.refs_2_ = f32[24,128]{1,0:T(8,128)} fusion(f32[1,128]{1,0:T(1,128)} %bitcast.19, f32[2,128]{1,0:T(2,128)} %param.21, f32[16,128]{1,0:T(8,128)} %bitcast.15, f32[24]{0:T(128)S(1)} %pad.3.clone), kind=kLoop, calls=%fused_computation | loop fusion | flops 9216 | bytes 22112 | tf_op jit(solution)/shard_map/concatenate | solution.py:561
  1.5 23.6 %gather_weights.1 = (bf16[512,1536]{1,0:T(8,128)(2,1)}, bf16[512,512]{1,0:T(8,128)(2,1)}, f32[4,24,128]{2,1,0:T(8,128)}) custom-call(bf16[128,1536]{1,0:T(8,128)(2,1)} %refs_0_.1, bf16[128,512]{1,0:T(8,128)(2,1)} %refs_1_.1, f32[24,128]{1,0:T(8,128)} %maximum_maximum_fusion.refs_2_), custom_call_target="tpu_custom_call" | custom-call | tf_op jit(solution)/shard_map/gather_weights/pallas_call | solution.py:377
  25.1 22.9 %attention.1 = (f32[1024,512]{1,0:T(8,128)}, bf16[1024,512]{1,0:T(8,128)(2,1)}) custom-call(bf16[1024,512]{1,0:T(8,128)(2,1)} %tok_ref.1, bf16[512,1536]{1,0:T(8,128)(2,1)} %get-tuple-element.10.wqkv_ref, bf16[512,512]{1,0:T(8,128)(2,1)} %get-tuple-element.11.wproj_ref, f32[4,24,128]{2,1,0:T(8,128)} %get-tuple-element.12.net_ref, ...), custom_call_target="tpu_custom_call" | custom-call | tf_op jit(solution)/shard_map/attention/pallas_call | solution.py:142
  48.0 0.0 copy-start.1
  48.0 0.0 copy-start.2
  48.0 0.0 copy-start.3
  48.0 0.0 copy-start.4
  48.0 0.0 copy-start.5
  48.0 32.4 %experts.1 = bf16[8,160,512]{2,1,0:T(8,128)(2,1)} custom-call(bf16[1024,512]{1,0:T(8,128)(2,1)} %get-tuple-element.14.refs_0_.normed_ref, s32[1,1024]{1,0:T(1,128)} %bitcast.10, s32[1,1024]{1,0:T(1,128)} %bitcast.12, bf16[2,512,2048]{2,1,0:T(8,128)(2,1)} %refs_3_.1, bf16[2,2048,512]{2,1,0:T(8,128)(2,1)} %refs_4_.1), custom_call_target="tpu_custom_call" | custom-call | tf_op jit(solution)/shard_map/experts/pallas_call | solution.py:530
  80.5 0.0 copy-done.1
  80.5 0.0 copy-done.2
  80.5 0.0 copy-done.3
  80.5 0.0 copy-done.4
  80.5 0.0 copy-done.5
  80.5 0.0 copy-start
  80.5 1.3 %copy-done = bf16[8,160,512]{2,1,0:T(8,128)(2,1)S(1)} copy-done((bf16[8,160,512]{2,1,0:T(8,128)(2,1)S(1)}, bf16[8,160,512]{2,1,0:T(8,128)(2,1)}, u32[]{:S(2)}) %copy-start) | copy-done | bytes 1310744
  81.8 3.2 %combine.1 = bf16[1024,512]{1,0:T(8,128)(2,1)} custom-call(f32[1024,512]{1,0:T(8,128)S(1)} %copy-done.2, bf16[1024,512]{1,0:T(8,128)(2,1)S(1)} %copy-done.1, bf16[8,512]{1,0:T(8,128)(2,1)S(1)} %bitcast.14, s32[1,1024]{1,0:T(1,128)S(1)} %bitcast.11, s32[1,1024]{1,0:T(1,128)S(1)} %bitcast.13, bf16[1280,512]{1,0:T(8,128)(2,1)S(1)} %bitcast.9), custom_call_target="tpu_custom_call" | custom-call | tf_op jit(solution)/shard_map/combine/pallas_call | solution.py:201
  (1 shorter events, 0.0 us)
Async XLA Ops:
  48.0 32.5 %copy-start.1 = (bf16[1024,512]{1,0:T(8,128)(2,1)S(1)}, bf16[1024,512]{1,0:T(8,128)(2,1)}, u32[]{:S(2)}) copy-start(bf16[1024,512]{1,0:T(8,128)(2,1)} %get-tuple-element.14.refs_0_.normed_ref) | copy-start | bytes 3145732
  48.0 32.5 %copy-start.2 = (f32[1024,512]{1,0:T(8,128)S(1)}, f32[1024,512]{1,0:T(8,128)}, u32[]{:S(2)}) copy-start(f32[1024,512]{1,0:T(8,128)} %get-tuple-element.13.res_ref) | copy-start | bytes 6291460
  48.0 32.5 %copy-start.3 = (s32[1024]{0:T(1024)S(1)}, s32[1024]{0:T(1024)}, u32[]{:S(2)}) copy-start(s32[1024]{0:T(1024)} %param.16) | copy-start | bytes 12292
  48.0 32.5 %copy-start.4 = (s32[1024]{0:T(1024)S(1)}, s32[1024]{0:T(1024)}, u32[]{:S(2)}) copy-start(s32[1024]{0:T(1024)} %param.17) | copy-start | bytes 12292
  48.0 32.5 %copy-start.5 = (bf16[512,8]{0,1:T(8,128)(2,1)S(1)}, bf16[512,8]{0,1:T(8,128)(2,1)}, u32[]{:S(2)}) copy-start(bf16[512,8]{0,1:T(8,128)(2,1)} %param.25) | copy-start | bytes 24580
  80.5 1.3 %copy-start = (bf16[8,160,512]{2,1,0:T(8,128)(2,1)S(1)}, bf16[8,160,512]{2,1,0:T(8,128)(2,1)}, u32[]{:S(2)}) copy-start(bf16[8,160,512]{2,1,0:T(8,128)(2,1)} %experts.1) | copy-start | bytes 3932164
